TPU v7x, 32 devices: a whole 2x2x4 slice. The times are simulated.
32 devices in a mesh: mem: 4 (over x, core), gx: 4 (over z), gy: 2 (over y).
Axes of the slice: x: 2, y: 2, z: 4, core: 2. Of those that a mesh axis runs over, the one named last changes fastest.
Arguments:
- perturbations: float32 [4, 32, 128, 512], P('mem', None, 'gx', 'gy'), may hold values from -9 to 9
- control: float32 [32, 128, 512], P(None, 'gx', 'gy'), may hold values from -6 to 6
Outputs:
- increment: float32 [32, 128, 512], P('mem', 'gx', 'gy')
All inputs are finite; a program needn't handle non-finite values.
Results may differ from a plain program's by a relative error of at most 0.0001.
Values sent between devices are 32-bit elements; how exact they have to be, the bound alone decides.
A program may use at most 64 MiB of HBM per device.

v0:
```python
import jax
import jax.numpy as jnp
from jax import lax
from jax.sharding import PartitionSpec as P


def padded_2(cells, sides, width):
    for axis, dim in sides:
        count = lax.axis_size(axis)
        ends = count - 1
        head = lax.slice_in_dim(cells, 0, width, axis=dim)
        tail = lax.slice_in_dim(cells, cells.shape[dim] - width, cells.shape[dim], axis=dim)
        cells = jnp.concatenate(
            [
                lax.ppermute(tail, axis, [(i, (i + 1) % count) for i in range(ends)]),
                cells,
                lax.ppermute(head, axis, [((i + 1) % count, i) for i in range(ends)]),
            ],
            axis=dim,
        )
    return cells


def tap_weights():
    offsets = jnp.arange(-4, 5).astype(jnp.float32)
    raw_taps = jnp.exp(-offsets * offsets / 18.0)
    return raw_taps / jnp.sqrt(jnp.sum(raw_taps * raw_taps))


def filter_padded(padded, margin, count_x, count_y):
    weights = tap_weights()
    begin_at = margin - 4
    along_x = sum(
        (
            weights[offset] * padded[:, :, begin_at + offset : begin_at + offset + count_x, :]
            for offset in range(9)
        )
    )
    return sum(
        (
            weights[offset] * along_x[:, :, :, begin_at + offset : begin_at + offset + count_y]
            for offset in range(9)
        )
    )


def restrict(values):
    shape_now = values.shape
    blocks = values.reshape(shape_now[:-2] + (shape_now[-2] // 2, 2, shape_now[-1] // 2, 2))
    return 0.5 * jnp.sum(blocks, axis=(-3, -1))


def prolong(coarse):
    return 0.5 * jnp.repeat(jnp.repeat(coarse, 2, axis=-2), 2, axis=-1)


def localize(values):
    count_x, count_y = (values.shape[2], values.shape[3])
    padded = padded_2(values, (("gx", 2), ("gy", 3)), 8)
    fine_part = filter_padded(padded, 8, count_x, count_y)
    coarse_part = filter_padded(restrict(padded), 4, count_x // 2, count_y // 2)
    return fine_part + prolong(coarse_part)


def body(perturbations, control):
    alpha = localize(localize(perturbations * control[None]))
    members_all = perturbations.shape[0] * lax.axis_size("mem")
    summed = lax.psum_scatter(
        jnp.sum(perturbations * alpha, axis=0), "mem", scatter_dimension=0, tiled=True
    )
    return summed / (members_all - 1)


def solution(mesh):
    placed = (P("mem", None, "gx", "gy"), P(None, "gx", "gy"))
    return jax.shard_map(
        body, mesh=mesh, in_specs=placed, out_specs=P("mem", "gx", "gy"), check_vma=False
    )
```

profile of v0, /device:TPU:0, one launch (start us, length us, event | category | flops | bytes accessed | tf_op | source)
XLA Modules:
  0.0 207.4 jit_solution(4558387186564659899)
XLA Ops:
  6.5 0.0 reduce-scatter.2.cloned.1.call-start
  6.5 1.7 bitcast_multiply_fusion
  8.3 4.9 %collective-permute-start = (f32[1,32,8,256]{3,2,1,0:T(8,128)S(1)}, f32[1,32,8,256]{3,2,1,0:T(8,128)S(1)}, u32[]{:S(2)}, u32[]{:S(2)}) collective-permute-start(f32[1,32,8,256]{3,2,1,0:T(8,128)S(1)} %get-tuple-element.11), channel_id=1, source_target_pairs={{0,2},{2,4},{4,6},{1,3},{3,5},{5,7},{8,10},{10,12},{12,14},{9,11},... | collective-permute-start | bytes 786440 | tf_op jit(solution)/shard_map/ppermute | solution.py:15
  13.2 1.3 collective-permute-start.1
  14.5 0.6 multiply_reduce_fusion
  15.9 2.9 %collective-permute-done = f32[1,32,8,256]{3,2,1,0:T(8,128)S(1)} collective-permute-done((f32[1,32,8,256]{3,2,1,0:T(8,128)S(1)}, f32[1,32,8,256]{3,2,1,0:T(8,128)S(1)}, u32[]{:S(2)}, u32[]{:S(2)}) %collective-permute-start) | collective-permute-done | bytes 262176 | tf_op jit(solution)/shard_map/ppermute | solution.py:15
  18.8 4.1 %collective-permute-done.1 = f32[1,32,8,256]{3,2,1,0:T(8,128)S(1)} collective-permute-done((f32[1,32,8,256]{3,2,1,0:T(8,128)S(1)}, f32[1,32,8,256]{3,2,1,0:T(8,128)S(1)}, u32[]{:S(2)}, u32[]{:S(2)}) %collective-permute-start.1) | collective-permute-done | bytes 262176 | tf_op jit(solution)/shard_map/ppermute | solution.py:17
  22.9 0.7 copy-done.4
  23.6 0.1 pad_maximum_fusion.2
  23.7 0.3 fusion.75
  24.0 0.2 copy.73
  24.2 0.3 copy.74
  24.5 1.3 collective-permute-start.3
  25.8 4.6 %collective-permute-start.2 = (f32[1,32,48,8]{2,3,1,0:T(8,128)S(1)}, f32[1,32,48,8]{2,3,1,0:T(8,128)S(1)}, u32[]{:S(2)}, u32[]{:S(2)}) collective-permute-start(f32[1,32,48,8]{2,3,1,0:T(8,128)S(1)} %copy.73), channel_id=1, source_target_pairs={{0,1},{2,3},{4,5},{6,7},{8,9},{10,11},{12,13},{14,15},{16,17},{18,... | collective-permute-start | bytes 147464 | tf_op jit(solution)/shard_map/ppermute | solution.py:15
  30.3 0.7 fusion.78
  31.0 1.8 collective-permute-done.2
  32.8 1.2 copy.59
  34.1 0.0 collective-permute-done.3
  34.1 1.2 copy.60
  35.2 2.4 %pad_maximum_fusion = f32[1,32,48,272]{3,2,1,0:T(8,128)S(1)} fusion(f32[1,32,48,8]{3,2,1,0:T(8,128)} %copy.60, f32[1,32,8,256]{3,2,1,0:T(8,128)} %copy-done.4, f32[1,32,32,256]{3,2,1,0:T(8,128)S(1)} %bitcast_multiply_fusion, f32[1,32,8,256]{3,2,1,0:T(8,128)} %copy-done.3, f32[1,32,48,8]{3,2,1,0:T(8,128)} %copy.59), kind=kLoop, calls=%fused_computation | loop fusion | flops 1671168 | bytes 3342336 | tf_op jit(solution)/shard_map/concatenate | solution.py:13
  37.6 4.5 %copy.61 = f32[1,32,48,272]{1,3,2,0:T(8,128)} copy(f32[1,32,48,272]{3,2,1,0:T(8,128)S(1)} %pad_maximum_fusion) | data formatting | bytes 3342336 | tf_op jit(solution)/shard_map/concatenate | solution.py:13
  42.2 9.6 %reduce_sum.30 = f32[32,24,136]{0,2,1:T(8,128)} reduce(f32[32,24,2,136,2]{0,4,3,2,1:T(2,128)} %bitcast.28, f32[]{:T(128)} %constant.3.clone.1), dimensions={2,4}, to_apply=%region_1.0 | reduce | flops 313344 | bytes 2088964 | tf_op jit(solution)/shard_map/reduce_sum | solution.py:50
  51.7 1.6 multiply_bitcast_fusion.1
  53.3 8.4 %fusion.8 = f32[1,32,32,272]{3,2,1,0:T(8,128)} fusion(f32[1,32,48,272]{3,2,1,0:T(8,128)S(1)} %pad_maximum_fusion, f32[]{:T(128)} %bitcast.9, f32[]{:T(128)} %bitcast.8, f32[]{:T(128)} %bitcast.7, f32[]{:T(128)} %bitcast.6, f32[]{:T(128)} %bitcast.5, f32[]{:T(128)} %bitcast.4, f32[]{:T(128)} %bitcast.3, f32[]{:T(128)} %bitcast.2, f32[]{:T(128)} %bitcast), kind=kLoop, calls=%fused_computation.22 | loop fusion | flops 4734976 | bytes 11141156 | tf_op jit(solution)/shard_map/add | solution.py:33
  61.7 6.1 %fusion.24 = f32[1,32,16,136]{1,3,2,0:T(8,128)S(1)} fusion(f32[1,32,24,136]{1,3,2,0:T(8,128)S(1)} %multiply_bitcast_fusion.1, f32[]{:T(128)} %bitcast.9, f32[]{:T(128)} %bitcast.8, f32[]{:T(128)} %bitcast.7, f32[]{:T(128)} %bitcast.6, f32[]{:T(128)} %bitcast.5, f32[]{:T(128)} %bitcast.4, f32[]{:T(128)} %bitcast.3, f32[]{:T(128)} %bitcast.2, f32[]{:T(128)} %bitcast), kind=kLoop, calls=%fused_computation.58 | loop fusion | flops 1183744 | bytes 2785316 | tf_op jit(solution)/shard_map/add | solution.py:33
  67.8 6.6 %fusion.55 = f32[32,16,128]{0,2,1:T(8,128)S(1)} fusion(f32[1,32,16,136]{1,3,2,0:T(8,128)S(1)} %fusion.24, f32[]{:T(128)} %bitcast.9, f32[]{:T(128)} %bitcast.8, f32[]{:T(128)} %bitcast.7, f32[]{:T(128)} %bitcast.6, f32[]{:T(128)} %bitcast.5, f32[]{:T(128)} %bitcast.4, f32[]{:T(128)} %bitcast.3, f32[]{:T(128)} %bitcast.2, f32[]{:T(128)} %bitcast), kind=kLoop, calls=%fused_computation.116 | loop fusion | flops 1179648 | bytes 2621476 | tf_op jit(solution)/shard_map/mul | solution.py:54
  74.4 0.3 copy.62
  74.7 0.1 broadcast_in_dim.16
  74.8 1.9 copy.63
  76.7 2.6 %broadcast_in_dim.17 = f32[32,32,128,2]{1,0,3,2:T(8,128)} broadcast(f32[32,32,128]{1,0,2:T(8,128)S(1)} %copy.63), dimensions={0,1,2} | broadcast | bytes 1572864 | tf_op jit(solution)/shard_map/broadcast_in_dim | solution.py:54
  79.3 4.9 %copy.64 = f32[1,32,32,256]{3,2,1,0:T(8,128)} copy(f32[1,32,32,256]{2,1,3,0:T(8,128)} %bitcast.29) | data formatting | bytes 2097152 | tf_op jit(solution)/shard_map/mul | solution.py:54
  84.2 9.2 %fusion.64 = f32[1,32,32,256]{3,2,1,0:T(8,128)S(1)} fusion(f32[1,32,32,256]{3,2,1,0:T(8,128)} %copy.64, f32[1,32,32,272]{3,2,1,0:T(8,128)S(1)} %copy-done.1, f32[]{:T(128)} %bitcast.9, f32[]{:T(128)} %bitcast.8, f32[]{:T(128)} %bitcast.7, f32[]{:T(128)} %bitcast.6, f32[]{:T(128)} %bitcast.5, f32[]{:T(128)} %bitcast.4, f32[]{:T(128)} %bitcast.3, f32[]{:T(128)} %bitcast.2, ...), kind=kLoop, calls=%fused_computation.134 | loop fusion | flops 4718592 | bytes 11534372 | tf_op jit(solution)/shard_map/add | solution.py:62
  93.5 3.5 %collective-permute-start.4 = (f32[1,32,8,256]{3,2,1,0:T(8,128)S(1)}, f32[1,32,8,256]{3,2,1,0:T(8,128)S(1)}, u32[]{:S(2)}, u32[]{:S(2)}) collective-permute-start(f32[1,32,8,256]{3,2,1,0:T(8,128)S(1)} %get-tuple-element.9), channel_id=1, source_target_pairs={{0,2},{2,4},{4,6},{1,3},{3,5},{5,7},{8,10},{10,12},{12,14},{9,11},... | collective-permute-start | bytes 786440 | tf_op jit(solution)/shard_map/ppermute | solution.py:15
  97.0 1.3 collective-permute-start.5
  98.3 2.6 %collective-permute-done.4 = f32[1,32,8,256]{3,2,1,0:T(8,128)S(1)} collective-permute-done((f32[1,32,8,256]{3,2,1,0:T(8,128)S(1)}, f32[1,32,8,256]{3,2,1,0:T(8,128)S(1)}, u32[]{:S(2)}, u32[]{:S(2)}) %collective-permute-start.4) | collective-permute-done | bytes 262176 | tf_op jit(solution)/shard_map/ppermute | solution.py:15
  100.8 4.4 %collective-permute-done.5 = f32[1,32,8,256]{3,2,1,0:T(8,128)S(1)} collective-permute-done((f32[1,32,8,256]{3,2,1,0:T(8,128)S(1)}, f32[1,32,8,256]{3,2,1,0:T(8,128)S(1)}, u32[]{:S(2)}, u32[]{:S(2)}) %collective-permute-start.5) | collective-permute-done | bytes 262176 | tf_op jit(solution)/shard_map/ppermute | solution.py:17
  105.2 0.1 pad_maximum_fusion.3
  105.4 0.6 copy-done.6
  105.9 0.3 fusion.74
  106.2 0.2 copy.65
  106.4 4.4 %collective-permute-start.6 = (f32[1,32,48,8]{2,3,1,0:T(8,128)S(1)}, f32[1,32,48,8]{2,3,1,0:T(8,128)S(1)}, u32[]{:S(2)}, u32[]{:S(2)}) collective-permute-start(f32[1,32,48,8]{2,3,1,0:T(8,128)S(1)} %copy.65), channel_id=1, source_target_pairs={{0,1},{2,3},{4,5},{6,7},{8,9},{10,11},{12,13},{14,15},{16,17},{18,... | collective-permute-start | bytes 147464 | tf_op jit(solution)/shard_map/ppermute | solution.py:15
  110.8 0.2 copy.66
  111.1 1.3 collective-permute-start.7
  112.4 0.9 collective-permute-done.6
  113.3 1.2 copy.67
  114.5 3.4 %collective-permute-done.7 = f32[1,32,48,8]{2,3,1,0:T(8,128)S(1)} collective-permute-done((f32[1,32,48,8]{2,3,1,0:T(8,128)S(1)}, f32[1,32,48,8]{2,3,1,0:T(8,128)S(1)}, u32[]{:S(2)}, u32[]{:S(2)}) %collective-permute-start.7) | collective-permute-done | bytes 49184 | tf_op jit(solution)/shard_map/ppermute | solution.py:17
  117.9 1.2 copy.68
  119.1 2.4 %pad_maximum_fusion.1 = f32[1,32,48,272]{3,2,1,0:T(8,128)S(1)} fusion(f32[1,32,48,8]{3,2,1,0:T(8,128)} %copy.68, f32[1,32,8,256]{3,2,1,0:T(8,128)} %copy-done.6, f32[1,32,32,256]{3,2,1,0:T(8,128)S(1)} %fusion.64, f32[1,32,8,256]{3,2,1,0:T(8,128)} %copy-done.5, f32[1,32,48,8]{3,2,1,0:T(8,128)} %copy.67), kind=kLoop, calls=%fused_computation.1 | loop fusion | flops 1671168 | bytes 3342336 | tf_op jit(solution)/shard_map/concatenate | solution.py:13
  121.5 8.4 %fusion = f32[1,32,32,272]{3,2,1,0:T(8,128)} fusion(f32[1,32,48,272]{3,2,1,0:T(8,128)S(1)} %pad_maximum_fusion.1, f32[]{:T(128)} %bitcast.9, f32[]{:T(128)} %bitcast.8, f32[]{:T(128)} %bitcast.7, f32[]{:T(128)} %bitcast.6, f32[]{:T(128)} %bitcast.5, f32[]{:T(128)} %bitcast.4, f32[]{:T(128)} %bitcast.3, f32[]{:T(128)} %bitcast.2, f32[]{:T(128)} %bitcast), kind=kLoop, calls=%fused_computation.5 | loop fusion | flops 4734976 | bytes 11141156 | tf_op jit(solution)/shard_map/add | solution.py:33
  129.9 4.4 %copy.69 = f32[1,32,48,272]{1,3,2,0:T(8,128)} copy(f32[1,32,48,272]{3,2,1,0:T(8,128)S(1)} %pad_maximum_fusion.1) | data formatting | bytes 3342336 | tf_op jit(solution)/shard_map/concatenate | solution.py:13
  134.3 8.3 %reduce_sum.34 = f32[32,24,136]{0,2,1:T(8,128)S(1)} reduce(f32[32,24,2,136,2]{0,4,3,2,1:T(2,128)} %bitcast.27, f32[]{:T(128)} %constant.3.clone.1), dimensions={2,4}, to_apply=%region_2.0 | reduce | flops 313344 | bytes 2088964 | tf_op jit(solution)/shard_map/reduce_sum | solution.py:50
  142.6 0.1 multiply_bitcast_fusion
  142.8 6.1 %fusion.16 = f32[1,32,16,136]{1,3,2,0:T(8,128)S(1)} fusion(f32[1,32,24,136]{1,3,2,0:T(8,128)S(1)} %multiply_bitcast_fusion, f32[]{:T(128)} %bitcast.9, f32[]{:T(128)} %bitcast.8, f32[]{:T(128)} %bitcast.7, f32[]{:T(128)} %bitcast.6, f32[]{:T(128)} %bitcast.5, f32[]{:T(128)} %bitcast.4, f32[]{:T(128)} %bitcast.3, f32[]{:T(128)} %bitcast.2, f32[]{:T(128)} %bitcast), kind=kLoop, calls=%fused_computation.41 | loop fusion | flops 1183744 | bytes 2785316 | tf_op jit(solution)/shard_map/add | solution.py:33
  148.9 6.6 %fusion.34 = f32[32,16,128]{0,2,1:T(8,128)S(1)} fusion(f32[1,32,16,136]{1,3,2,0:T(8,128)S(1)} %fusion.16, f32[]{:T(128)} %bitcast.9, f32[]{:T(128)} %bitcast.8, f32[]{:T(128)} %bitcast.7, f32[]{:T(128)} %bitcast.6, f32[]{:T(128)} %bitcast.5, f32[]{:T(128)} %bitcast.4, f32[]{:T(128)} %bitcast.3, f32[]{:T(128)} %bitcast.2, f32[]{:T(128)} %bitcast), kind=kLoop, calls=%fused_computation.77 | loop fusion | flops 1179648 | bytes 2621476 | tf_op jit(solution)/shard_map/mul | solution.py:54
  155.5 0.3 copy.70
  155.8 0.1 broadcast_in_dim.18
  155.9 1.9 copy.71
  157.8 2.6 %broadcast_in_dim.19 = f32[32,32,128,2]{1,0,3,2:T(8,128)} broadcast(f32[32,32,128]{1,0,2:T(8,128)S(1)} %copy.71), dimensions={0,1,2} | broadcast | bytes 1572864 | tf_op jit(solution)/shard_map/broadcast_in_dim | solution.py:54
  160.4 4.7 %copy.72 = f32[1,32,32,256]{3,2,1,0:T(8,128)} copy(f32[1,32,32,256]{2,1,3,0:T(8,128)} %bitcast.30) | data formatting | bytes 2097152 | tf_op jit(solution)/shard_map/mul | solution.py:54
  165.1 0.0 copy-done
  165.1 10.2 %fusion.45 = f32[32,32,256]{2,1,0:T(8,128)} fusion(f32[1,32,32,256]{3,2,1,0:T(8,128)S(1)} %copy-done.2, f32[1,32,32,256]{3,2,1,0:T(8,128)} %copy.72, f32[1,32,32,272]{3,2,1,0:T(8,128)S(1)} %copy-done, f32[]{:T(128)} %bitcast.9, f32[]{:T(128)} %bitcast.8, f32[]{:T(128)} %bitcast.7, f32[]{:T(128)} %bitcast.6, f32[]{:T(128)} %bitcast.5, f32[]{:T(128)} %bitcast.4, ...), kind=kLoop, calls=%fused_computation.97 | loop fusion | flops 4980736 | bytes 12582948 | tf_op jit(solution)/shard_map/reduce_sum | solution.py:69
  175.4 0.0 reduce-scatter.2.cloned.1.call-update
  175.4 23.3 %reduce-scatter.2.cloned.1.call-done = f32[8,32,256]{2,1,0:T(8,128)} async-done(((f32[32,32,256]{2,1,0:T(8,128)}), f32[8,32,256]{2,1,0:T(8,128)}) %reduce-scatter.2.cloned.1.call-update) | async-done | bytes 262160 | tf_op jit(solution)/shard_map/reduce_scatter | solution.py:68
  198.7 1.7 broadcast_multiply_fusion
  (14 shorter events, 0.1 us)
Async XLA Ops:
  6.5 192.1 %reduce-scatter.2.cloned.1.call-start = ((), (), s32[]{:S(2)}) async-start(), calls=%async_computation.1 | async-start | bytes 1310720 | tf_op jit(solution)/shard_map/reduce_scatter | solution.py:68
  8.3 10.5 %collective-permute-start = (f32[1,32,8,256]{3,2,1,0:T(8,128)S(1)}, f32[1,32,8,256]{3,2,1,0:T(8,128)S(1)}, u32[]{:S(2)}, u32[]{:S(2)}) collective-permute-start(f32[1,32,8,256]{3,2,1,0:T(8,128)S(1)} %get-tuple-element.11), channel_id=1, source_target_pairs={{0,2},{2,4},{4,6},{1,3},{3,5},{5,7},{8,10},{10,12},{12,14},{9,11},... | collective-permute-start | bytes 786440 | tf_op jit(solution)/shard_map/ppermute | solution.py:15
  13.2 9.7 %collective-permute-start.1 = (f32[1,32,8,256]{3,2,1,0:T(8,128)S(1)}, f32[1,32,8,256]{3,2,1,0:T(8,128)S(1)}, u32[]{:S(2)}, u32[]{:S(2)}) collective-permute-start(f32[1,32,8,256]{3,2,1,0:T(8,128)S(1)} %get-tuple-element.12), channel_id=1, source_target_pairs={{2,0},{4,2},{6,4},{3,1},{5,3},{7,5},{10,8},{12,10},{14,12},{11,9},... | collective-permute-start | bytes 786440 | tf_op jit(solution)/shard_map/ppermute | solution.py:17
  18.8 4.1 %copy-start.3 = (f32[1,32,8,256]{3,2,1,0:T(8,128)}, f32[1,32,8,256]{3,2,1,0:T(8,128)S(1)}, u32[]{:S(2)}) copy-start(f32[1,32,8,256]{3,2,1,0:T(8,128)S(1)} %collective-permute-done) | copy-start | bytes 786436
  22.9 0.7 copy-start.4
  24.5 9.6 %collective-permute-start.3 = (f32[1,32,48,8]{2,3,1,0:T(8,128)S(1)}, f32[1,32,48,8]{2,3,1,0:T(8,128)S(1)}, u32[]{:S(2)}, u32[]{:S(2)}) collective-permute-start(f32[1,32,48,8]{2,3,1,0:T(8,128)S(1)} %copy.74), channel_id=1, source_target_pairs={{1,0},{3,2},{5,4},{7,6},{9,8},{11,10},{13,12},{15,14},{17,16},{19,... | collective-permute-start | bytes 147464 | tf_op jit(solution)/shard_map/ppermute | solution.py:17
  25.8 7.1 %collective-permute-start.2 = (f32[1,32,48,8]{2,3,1,0:T(8,128)S(1)}, f32[1,32,48,8]{2,3,1,0:T(8,128)S(1)}, u32[]{:S(2)}, u32[]{:S(2)}) collective-permute-start(f32[1,32,48,8]{2,3,1,0:T(8,128)S(1)} %copy.73), channel_id=1, source_target_pairs={{0,1},{2,3},{4,5},{6,7},{8,9},{10,11},{12,13},{14,15},{16,17},{18,... | collective-permute-start | bytes 147464 | tf_op jit(solution)/shard_map/ppermute | solution.py:15
  79.3 4.9 %copy-start.1 = (f32[1,32,32,272]{3,2,1,0:T(8,128)S(1)}, f32[1,32,32,272]{3,2,1,0:T(8,128)}, u32[]{:S(2)}) copy-start(f32[1,32,32,272]{3,2,1,0:T(8,128)} %fusion.8) | copy-start | bytes 3342340
  93.5 7.3 %collective-permute-start.4 = (f32[1,32,8,256]{3,2,1,0:T(8,128)S(1)}, f32[1,32,8,256]{3,2,1,0:T(8,128)S(1)}, u32[]{:S(2)}, u32[]{:S(2)}) collective-permute-start(f32[1,32,8,256]{3,2,1,0:T(8,128)S(1)} %get-tuple-element.9), channel_id=1, source_target_pairs={{0,2},{2,4},{4,6},{1,3},{3,5},{5,7},{8,10},{10,12},{12,14},{9,11},... | collective-permute-start | bytes 786440 | tf_op jit(solution)/shard_map/ppermute | solution.py:15
  97.0 8.3 %collective-permute-start.5 = (f32[1,32,8,256]{3,2,1,0:T(8,128)S(1)}, f32[1,32,8,256]{3,2,1,0:T(8,128)S(1)}, u32[]{:S(2)}, u32[]{:S(2)}) collective-permute-start(f32[1,32,8,256]{3,2,1,0:T(8,128)S(1)} %get-tuple-element.10), channel_id=1, source_target_pairs={{2,0},{4,2},{6,4},{3,1},{5,3},{7,5},{10,8},{12,10},{14,12},{11,9},... | collective-permute-start | bytes 786440 | tf_op jit(solution)/shard_map/ppermute | solution.py:17
  100.8 4.5 %copy-start.5 = (f32[1,32,8,256]{3,2,1,0:T(8,128)}, f32[1,32,8,256]{3,2,1,0:T(8,128)S(1)}, u32[]{:S(2)}) copy-start(f32[1,32,8,256]{3,2,1,0:T(8,128)S(1)} %collective-permute-done.4) | copy-start | bytes 786436
  105.2 0.7 copy-start.6
  106.4 6.9 %collective-permute-start.6 = (f32[1,32,48,8]{2,3,1,0:T(8,128)S(1)}, f32[1,32,48,8]{2,3,1,0:T(8,128)S(1)}, u32[]{:S(2)}, u32[]{:S(2)}) collective-permute-start(f32[1,32,48,8]{2,3,1,0:T(8,128)S(1)} %copy.65), channel_id=1, source_target_pairs={{0,1},{2,3},{4,5},{6,7},{8,9},{10,11},{12,13},{14,15},{16,17},{18,... | collective-permute-start | bytes 147464 | tf_op jit(solution)/shard_map/ppermute | solution.py:15
  111.1 6.9 %collective-permute-start.7 = (f32[1,32,48,8]{2,3,1,0:T(8,128)S(1)}, f32[1,32,48,8]{2,3,1,0:T(8,128)S(1)}, u32[]{:S(2)}, u32[]{:S(2)}) collective-permute-start(f32[1,32,48,8]{2,3,1,0:T(8,128)S(1)} %copy.66), channel_id=1, source_target_pairs={{1,0},{3,2},{5,4},{7,6},{9,8},{11,10},{13,12},{15,14},{17,16},{19,... | collective-permute-start | bytes 147464 | tf_op jit(solution)/shard_map/ppermute | solution.py:17
  160.4 4.7 %copy-start = (f32[1,32,32,272]{3,2,1,0:T(8,128)S(1)}, f32[1,32,32,272]{3,2,1,0:T(8,128)}, u32[]{:S(2)}) copy-start(f32[1,32,32,272]{3,2,1,0:T(8,128)} %fusion) | copy-start | bytes 3342340
  160.4 4.7 %copy-start.2 = (f32[1,32,32,256]{3,2,1,0:T(8,128)S(1)}, f32[1,32,32,256]{3,2,1,0:T(8,128)}, u32[]{:S(2)}) copy-start(f32[1,32,32,256]{3,2,1,0:T(8,128)} %param.2) | copy-start | bytes 3145732
Sparse Core Ops, SparseCore 0:
  175.5 23.1 reduce-scatter.1
where the time goes:
time: 211 us; the launch traced here: 207 us
  other arithmetic  90.3 us (43%)
  waiting for transfers between devices  43.5 us (21%)
  local copies, waits for them, and re-layouts  36.5 us (17%)
  starting transfers between devices  22.6 us (11%)
  between operations  14.6 us (7%)
    add x4, other arithmetic, filter_padded(): sum((weights[offset] * padded[:, :, begin_at + offset:begin_at + offset +...  29 us
    reduce_scatter x1, waiting for transfers between devices, body(): lax.psum_scatter(jnp.sum(perturbations * alpha, axis=0), 'mem', scatter_d...  23.3 us
    reduce_sum x2, other arithmetic, restrict(): return 0.5 * jnp.sum(blocks, axis=(-3, -1))  17.9 us
    ppermute x4, starting transfers between devices, padded_2(): lax.ppermute(tail, axis, [(i, (i + 1) % count) for i in range(ends)])  17.4 us
    mul x6, local copies, waits for them, and re-layouts, prolong(): return 0.5 * jnp.repeat(jnp.repeat(coarse, 2, axis=-2), 2, axis=-1)  14 us
    mul x2, other arithmetic, prolong(): return 0.5 * jnp.repeat(jnp.repeat(coarse, 2, axis=-2), 2, axis=-1)  13.2 us
    ppermute x4, waiting for transfers between devices, padded_2(): lax.ppermute(head, axis, [((i + 1) % count, i) for i in range(ends)])  11.9 us
    reduce_sum x1, other arithmetic, body(): jnp.sum(perturbations * alpha, axis=0)  10.2 us
  transfers between devices with their start and end apart: 9, of which 8 were waited for; matrix products, arithmetic and copies ran while one was open for 2% of the time, Pallas kernels for 0%

commit v1 on v0

v1 whole, which is shorter than its diff:
```python
import functools
import math

import jax
import jax.numpy as jnp
import ml_dtypes
import numpy as np
from jax import lax
from jax.experimental import pallas as pl
from jax.experimental.pallas import tpu as pltpu
from jax.sharding import PartitionSpec as P

MESH = pl.DeviceIdType.MESH
REACH = 16
GROUP = 8
LANES = 128


def smoothing(n):
    o = np.arange(-4, 5).astype(np.float64)
    taps = np.exp(-o * o / 18.0)
    taps = taps / np.sqrt(np.sum(taps * taps))
    a = np.zeros((n, n))
    for k, t in zip(range(-4, 5), taps):
        a += t * np.eye(n, k=k)
    return a


def four_terms(n):
    a = smoothing(n)
    r = np.kron(np.eye(n // 2), np.ones((1, 2))) / math.sqrt(2.0)
    b = r.T @ smoothing(n // 2) @ r
    return [a @ a, a @ b, b @ a, b @ b]


def split_np(m):
    hi = m.astype(np.float32).astype(ml_dtypes.bfloat16)
    lo = (m - hi.astype(np.float64)).astype(np.float32).astype(ml_dtypes.bfloat16)
    return hi, lo


def constants(nx, ny, gx, gy):
    rows, cols = nx // gx, ny // gy
    xs = []
    for g in range(gx):
        blocks = []
        for m in four_terms(nx):
            wide = np.pad(m, ((0, 0), (REACH, REACH)))
            blocks.append(wide[g * rows : (g + 1) * rows, g * rows : (g + 1) * rows + 2 * REACH])
        hi, lo = split_np(np.concatenate(blocks, 0))
        xs.append(np.concatenate([hi, lo, hi], 1))
    ys, hs = [], []
    for g in range(gy):
        own, edge = [], []
        for m in four_terms(ny):
            mine = m[g * cols : (g + 1) * cols]
            own.append(mine[:, g * cols : (g + 1) * cols].T)
            if g == 0:
                part = mine[cols - REACH :, cols : cols + REACH].T
            else:
                part = mine[:REACH, g * cols - REACH : g * cols].T
            block = np.zeros((LANES, LANES))
            for s in range(GROUP):
                before = (s + GROUP - 1) % GROUP
                slot_in, slot_out = (s, before) if g == 0 else (before, s)
                block[slot_in * REACH :][:REACH, slot_out * REACH : (slot_out + 1) * REACH] = part
            edge.append(block)
        ys.append(np.stack(split_np(np.concatenate(own, 0))))
        hs.append(np.stack(split_np(np.concatenate(edge, 0))))
    return np.stack(xs), np.stack(ys), np.stack(hs)


def split(v):
    hi = v.astype(jnp.bfloat16)
    return hi, (v - hi.astype(jnp.float32)).astype(jnp.bfloat16)


def dot(a, b):
    return jnp.dot(a, b, preferred_element_type=jnp.float32)


def kernel(
    gx_n, scale, chunks, per_chunk,
    p_hbm, c_hbm, x_hbm, y_hbm, h_hbm, out_hbm,
    p, c, f, pk, hk, xm, ym, hm, con, ra, rb, ob,
    ld, kd, zs, zr, ds, dr, as_, ar, bs, br, od,
):
    half = p.shape[0]
    rows, cols = p.shape[3], p.shape[4]
    mem, gx, gy = lax.axis_index("mem"), lax.axis_index("gx"), lax.axis_index("gy")
    chip, core = lax.div(mem, 2), lax.rem(mem, 2)
    other = 1 - gy

    def part(k):
        return pl.ds(k * per_chunk, per_chunk)

    def loads(k):
        return [
            pltpu.make_async_copy(src.at[:, :, part(k)], dst.at[:, :, part(k)], ld.at[k, n])
            for n, (src, dst) in enumerate(((p_hbm, p), (c_hbm, c)))
        ]

    def const_loads():
        return [
            pltpu.make_async_copy(x_hbm.at[gx], xm, kd.at[0]),
            pltpu.make_async_copy(y_hbm.at[gy], ym, kd.at[1]),
            pltpu.make_async_copy(h_hbm.at[gy], hm, kd.at[2]),
        ]

    for k in range(chunks):
        for copy in loads(k):
            copy.start()
    for copy in const_loads():
        copy.start()

    barrier = pltpu.get_barrier_semaphore()
    greet = lambda where: pl.semaphore_signal(barrier, inc=1, device_id=where, device_id_type=MESH)
    greet({"gy": other})
    greet({"mem": chip * 2 + 1 - core})
    for k in range(1, half):
        greet({"mem": lax.rem(chip + k, half) * 2 + core})

    @pl.when(gx > 0)
    def _():
        greet({"gx": gx - 1})
        greet({"gx": gx - 1, "gy": other})

    @pl.when(gx < gx_n - 1)
    def _():
        greet({"gx": gx + 1})
        greet({"gx": gx + 1, "gy": other})

    @pl.when(gx == 0)
    def _():
        f[:, :, :, 0:REACH] = jnp.zeros_like(f[:, :, :, 0:REACH])
        hk[:, :, 0:REACH] = jnp.zeros_like(hk[:, :, 0:REACH])

    @pl.when(gx == gx_n - 1)
    def _():
        f[:, :, :, rows + REACH :] = jnp.zeros_like(f[:, :, :, rows + REACH :])
        hk[:, :, rows + REACH :] = jnp.zeros_like(hk[:, :, rows + REACH :])

    pl.semaphore_wait(
        barrier,
        half + 1 + 2 * jnp.where(gx > 0, 1, 0) + 2 * jnp.where(gx < gx_n - 1, 1, 0),
    )

    low, high = pl.ds(0, REACH), pl.ds(rows + REACH, REACH)
    first, last = pl.ds(REACH, REACH), pl.ds(rows, REACH)

    def remote(src, dst, ss, rs, where):
        return pltpu.make_async_remote_copy(
            src_ref=src, dst_ref=dst, send_sem=ss, recv_sem=rs, device_id=where, device_id_type=MESH
        )

    def side(k):
        return remote(
            pk.at[k], hk.at[k, :, pl.ds(REACH, rows)], ds.at[k, 0], dr.at[k, 0], {"gy": other}
        )

    def down(k):
        return (
            remote(f.at[:, :, part(k), first], f.at[:, :, part(k), high], zs.at[k, 0], zr.at[k, 0], {"gx": gx - 1}),
            remote(pk.at[k, :, pl.ds(0, REACH)], hk.at[k, :, high], ds.at[k, 1], dr.at[k, 1], {"gx": gx - 1, "gy": other}),
        )

    def up(k):
        return (
            remote(f.at[:, :, part(k), last], f.at[:, :, part(k), low], zs.at[k, 1], zr.at[k, 1], {"gx": gx + 1}),
            remote(pk.at[k, :, pl.ds(rows - REACH, REACH)], hk.at[k, :, low], ds.at[k, 2], dr.at[k, 2], {"gx": gx + 1, "gy": other}),
        )

    members = [(i, b, j) for j in range(per_chunk) for i in range(half) for b in range(2)]
    groups = [members[n : n + GROUP] for n in range(0, len(members), GROUP)]
    slot = lax.broadcasted_iota(jnp.int32, (rows, LANES), 1) // REACH
    moved = jnp.where(gy == 0, GROUP - 1, 0)

    def send(k, carry):
        for copy in loads(k):
            copy.wait()
        for n, group in enumerate(groups):
            packed = jnp.zeros((rows, LANES), jnp.float32)
            for s, (i, b, j) in enumerate(group):
                at = k * per_chunk + j
                v = p[i, b, at] * c[i, b, at]
                f[i, b, at, pl.ds(REACH, rows)] = v
                edge = jnp.where(gy == 0, v[:, cols - LANES :], v[:, :LANES])
                if s:
                    edge = pltpu.roll(edge, s * REACH, 1)
                packed = jnp.where(slot == lax.rem(s + moved, GROUP), edge, packed)
            pk[k, n] = packed

        @pl.when(gx > 0)
        def _():
            for copy in down(k):
                copy.start()

        @pl.when(gx < gx_n - 1)
        def _():
            for copy in up(k):
                copy.start()

        side(k).start()
        return carry

    lax.fori_loop(0, chunks, send, 0)
    for copy in const_loads():
        copy.wait()

    def to_core(k):
        return remote(
            con.at[:, 1 - core, part(k)], ra.at[:, part(k)], as_.at[k], ar.at[k], {"mem": chip * 2 + 1 - core}
        )

    def to_chip(k, n):
        to = lax.rem(chip + n, half)
        return remote(
            ra.at[to, part(k)], rb.at[n - 1, part(k)], bs.at[k, n - 1], br.at[k, n - 1], {"mem": to * 2 + core}
        )

    def filtered(k):
        @pl.when(gx < gx_n - 1)
        def _():
            for copy in down(k):
                copy.wait_recv()

        @pl.when(gx > 0)
        def _():
            for copy in up(k):
                copy.wait_recv()

        side(k).wait_recv()
        x = xm[...]
        for n, group in enumerate(groups):
            his, los = [], []

            def along_x(v):
                hi, lo = split(v)
                g = dot(x, jnp.concatenate([hi, hi, lo], 0))
                g = jnp.concatenate([g[t * rows : (t + 1) * rows] for t in range(4)], 1)
                return split(g)

            for i, b, j in group:
                hi, lo = along_x(f[i, b, k * per_chunk + j])
                his.append(hi)
                los.append(lo)
            hi, lo = jnp.concatenate(his, 0), jnp.concatenate(los, 0)
            res = dot(hi, ym[0]) + dot(lo, ym[0]) + dot(hi, ym[1])
            hi, lo = along_x(hk[k, n])
            edge = dot(hi, hm[0]) + dot(lo, hm[0]) + dot(hi, hm[1])
            for s, (i, b, j) in enumerate(group):
                at = k * per_chunk + j
                r = res[s * rows : (s + 1) * rows]
                e = pltpu.roll(edge, LANES - s * REACH, 1) if s else edge
                left = jnp.where((slot == 0) & (gy == 1), e, 0.0)
                right = jnp.where((slot == GROUP - 1) & (gy == 0), e, 0.0)
                con[i, b, at, :, :LANES] = p[i, b, at, :, :LANES] * (r[:, :LANES] + left)
                if cols > 2 * LANES:
                    mid = pl.ds(LANES, cols - 2 * LANES)
                    con[i, b, at, :, mid] = p[i, b, at, :, mid] * r[:, LANES : cols - LANES]
                con[i, b, at, :, cols - LANES :] = p[i, b, at, :, cols - LANES :] * (r[:, cols - LANES :] + right)
        to_core(k).start()

    def summed(k):
        to_core(k).wait_recv()
        for n in range(1, half):
            to = lax.rem(chip + n, half)
            ra[to, part(k)] += con[to, core, part(k)]
            to_chip(k, n).start()

    def body(k, carry):
        filtered(k)

        @pl.when(k > 0)
        def _():
            summed(k - 1)

        return carry

    lax.fori_loop(0, chunks, body, 0)
    summed(chunks - 1)

    def finish(k, carry):
        total = con[chip, core, part(k)] + ra[chip, part(k)]
        for n in range(1, half):
            to_chip(k, n).wait_recv()
            total = total + rb[n - 1, part(k)]
        ob[part(k)] = total * scale
        pltpu.make_async_copy(ob.at[part(k)], out_hbm.at[part(k)], od.at[k]).start()
        return carry

    lax.fori_loop(0, chunks, finish, 0)

    def drain(k, carry):
        @pl.when(gx > 0)
        def _():
            for copy in down(k):
                copy.wait_send()

        @pl.when(gx < gx_n - 1)
        def _():
            for copy in up(k):
                copy.wait_send()

        side(k).wait_send()
        to_core(k).wait_send()
        for n in range(1, half):
            to_chip(k, n).wait_send()
        pltpu.make_async_copy(ob.at[part(k)], out_hbm.at[part(k)], od.at[k]).wait()
        return carry

    lax.fori_loop(0, chunks, drain, 0)


def body(perturbations, control):
    mem, gx, gy = (lax.axis_size(a) for a in ("mem", "gx", "gy"))
    members, fields, rows, cols = perturbations.shape
    assert members == 1 and gy == 2 and mem % 2 == 0 and rows >= REACH and cols >= 2 * LANES
    half, per = mem // 2, fields // mem
    per_chunk = next(n for n in range(1, per + 1) if per % n == 0 and mem * n % GROUP == 0)
    chunks = per // per_chunk
    n_groups = mem * per_chunk // GROUP
    xm, ym, hm = constants(rows * gx, cols * gy, gx, gy)
    shape = (half, 2, per, rows, cols)
    tall = rows + 2 * REACH
    f32 = jnp.float32
    any_ = pl.BlockSpec(memory_space=pl.ANY)
    dma = pltpu.SemaphoreType.DMA
    n_to = max(half - 1, 1)
    out = pl.pallas_call(
        functools.partial(kernel, gx, 1.0 / (mem * members - 1), chunks, per_chunk),
        out_shape=jax.ShapeDtypeStruct((per, rows, cols), f32),
        in_specs=[any_] * 5,
        out_specs=any_,
        scratch_shapes=[
            pltpu.VMEM(shape, f32),
            pltpu.VMEM(shape, f32),
            pltpu.VMEM((half, 2, per, tall, cols), f32),
            pltpu.VMEM((chunks, n_groups, rows, LANES), f32),
            pltpu.VMEM((chunks, n_groups, tall, LANES), f32),
            pltpu.VMEM(xm.shape[1:], jnp.bfloat16),
            pltpu.VMEM(ym.shape[1:], jnp.bfloat16),
            pltpu.VMEM(hm.shape[1:], jnp.bfloat16),
            pltpu.VMEM(shape, f32),
            pltpu.VMEM((half, per, rows, cols), f32),
            pltpu.VMEM((n_to, per, rows, cols), f32),
            pltpu.VMEM((per, rows, cols), f32),
            dma((chunks, 2)),
            dma((3,)),
            dma((chunks, 2)),
            dma((chunks, 2)),
            dma((chunks, 3)),
            dma((chunks, 3)),
            dma((chunks,)),
            dma((chunks,)),
            dma((chunks, n_to)),
            dma((chunks, n_to)),
            dma((chunks,)),
        ],
        compiler_params=pltpu.CompilerParams(
            collective_id=0, has_side_effects=True, vmem_limit_bytes=40 * 1024 * 1024
        ),
        cost_estimate=pl.CostEstimate(flops=10**10, bytes_accessed=4 * 2**20, transcendentals=0),
    )(
        perturbations.reshape(shape),
        control.reshape(shape),
        jnp.asarray(xm),
        jnp.asarray(ym),
        jnp.asarray(hm),
    )
    return out


def solution(mesh):
    placed = (P("mem", None, "gx", "gy"), P(None, "gx", "gy"))
    return jax.shard_map(
        body, mesh=mesh, in_specs=placed, out_specs=P("mem", "gx", "gy"), check_vma=False
    )
```

time: 211 us -> 32.3 us (0.15); the launches traced: 207 us -> 32.1 us
  other arithmetic: 90.3 us -> 0 us
  waiting for transfers between devices: 43.5 us -> 0 us
  local copies, waits for them, and re-layouts: 36.5 us -> 6.73 us
  Pallas kernels: 0 us -> 25.3 us
  starting transfers between devices: 22.6 us -> 0 us
  between operations: 14.6 us -> 0.01 us
    add x5 -> x0, other arithmetic: 38.3 us -> none  [the longest x4 29 us: filter_padded(): sum((weights[offset] * padded[:, :, begin_at + offset:begin_at + offset +...]
    reduce_sum x4 -> x0, other arithmetic: 28.7 us -> none  [the longest x2 17.9 us: restrict(): return 0.5 * jnp.sum(blocks, axis=(-3, -1))]
    pallas_call x0 -> x1, Pallas kernels: none -> 25.3 us  [body(): pl.pallas_call(functools.partial(kernel, gx, 1.0 / (mem * members - 1), c...]
    reduce_scatter x1 -> x0, waiting for transfers between devices: 23.3 us -> none  [body(): lax.psum_scatter(jnp.sum(perturbations * alpha, axis=0), 'mem', scatter_d...]
    ppermute x8 -> x0, starting transfers between devices: 22.6 us -> none  [the longest x4 17.4 us: padded_2(): lax.ppermute(tail, axis, [(i, (i + 1) % count) for i in range(ends)])]
    ppermute x8 -> x0, waiting for transfers between devices: 20.2 us -> none  [the longest x4 11.9 us: padded_2(): lax.ppermute(head, axis, [((i + 1) % count, i) for i in range(ends)])]
    mul x5 -> x0, other arithmetic: 16.6 us -> none  [the longest x2 13.2 us: prolong(): return 0.5 * jnp.repeat(jnp.repeat(coarse, 2, axis=-2), 2, axis=-1)]
    mul x6 -> x0, local copies, waits for them, and re-layouts: 14 us -> none  [prolong(): return 0.5 * jnp.repeat(jnp.repeat(coarse, 2, axis=-2), 2, axis=-1)]
  transfers between devices with their start and end apart: 9 -> 0, of which waited for: 8 -> 0; matrix products, arithmetic and copies ran while one was open for 2% -> 0% of each run, Pallas kernels for 0% -> 0%
where the time goes in v1:
time: 32.3 us; the launch traced here: 32.1 us
  Pallas kernels  25.3 us (78%)
  local copies, waits for them, and re-layouts  6.73 us (21%)
    pallas_call x1, Pallas kernels, body(): pl.pallas_call(functools.partial(kernel, gx, 1.0 / (mem * members - 1), c...  25.3 us
    unnamed x11, local copies, waits for them, and re-layouts  6.73 us

profile of v1, /device:TPU:0, one launch (start us, length us, event | category | flops | bytes accessed | tf_op | source)
XLA Modules:
  0.0 32.1 jit_solution(15457742647559471964)
XLA Ops:
  0.0 0.0 copy-start
  0.0 1.2 %copy-done = f32[1,32,32,256]{3,2,1,0:T(8,128)S(1)} copy-done((f32[1,32,32,256]{3,2,1,0:T(8,128)S(1)}, f32[1,32,32,256]{3,2,1,0:T(8,128)}, u32[]{:S(2)}) %copy-start) | copy-done | bytes 1048600
  1.2 0.0 copy-start.1
  1.2 1.2 %copy-done.1 = f32[32,32,256]{2,1,0:T(8,128)S(1)} copy-done((f32[32,32,256]{2,1,0:T(8,128)S(1)}, f32[32,32,256]{2,1,0:T(8,128)}, u32[]{:S(2)}) %copy-start.1) | copy-done | bytes 1048600
  2.5 0.0 copy-start.2
  2.5 1.6 %copy-done.2 = bf16[2,2,1024,256]{3,2,1,0:T(8,128)(2,1)S(1)} copy-done((bf16[2,2,1024,256]{3,2,1,0:T(8,128)(2,1)S(1)}, bf16[2,2,1024,256]{3,2,1,0:T(8,128)(2,1)}, u32[]{:S(2)}) %copy-start.2) | copy-done | bytes 2097176
  4.0 0.0 copy-start.3
  4.0 1.0 %copy-done.3 = bf16[2,2,512,128]{3,2,1,0:T(8,128)(2,1)S(1)} copy-done((bf16[2,2,512,128]{3,2,1,0:T(8,128)(2,1)S(1)}, bf16[2,2,512,128]{3,2,1,0:T(8,128)(2,1)}, u32[]{:S(2)}) %copy-start.3) | copy-done | bytes 524312
  5.1 0.0 copy-start.4
  5.1 0.9 %copy-done.4 = bf16[4,128,192]{2,1,0:T(8,128)(2,1)S(1)} copy-done((bf16[4,128,192]{2,1,0:T(8,128)(2,1)S(1)}, bf16[4,128,192]{2,1,0:T(8,128)(2,1)}, u32[]{:S(2)}) %copy-start.4) | copy-done | bytes 196632
  6.0 25.3 %shard_map.55 = f32[8,32,256]{2,1,0:T(8,128)S(1)} custom-call(f32[2,2,8,32,256]{4,3,2,1,0:T(8,128)S(1)} %bitcast.2, f32[2,2,8,32,256]{4,3,2,1,0:T(8,128)S(1)} %bitcast.3, bf16[4,128,192]{2,1,0:T(8,128)(2,1)S(1)} %copy-done.4, bf16[2,2,1024,256]{3,2,1,0:T(8,128)(2,1)S(1)} %copy-done.2, bf16[2,2,512,128]{3,2,1,0:T(8,128)(2,1)S(1)} %copy-done.3), custom_call_target="tpu_custom_call" | custom-call | flops 10000000000 | bytes 4194304 | tf_op jit(solution)/shard_map/pallas_call | solution.py:330
  31.3 0.7 %copy.7 = f32[8,32,256]{2,1,0:T(8,128)} copy(f32[8,32,256]{2,1,0:T(8,128)S(1)} %shard_map.55) | data formatting | bytes 524288
Async XLA Ops:
  0.0 1.2 %copy-start = (f32[1,32,32,256]{3,2,1,0:T(8,128)S(1)}, f32[1,32,32,256]{3,2,1,0:T(8,128)}, u32[]{:S(2)}) copy-start(f32[1,32,32,256]{3,2,1,0:T(8,128)} %param.5) | copy-start | bytes 3145732
  1.2 1.2 %copy-start.1 = (f32[32,32,256]{2,1,0:T(8,128)S(1)}, f32[32,32,256]{2,1,0:T(8,128)}, u32[]{:S(2)}) copy-start(f32[32,32,256]{2,1,0:T(8,128)} %param.6) | copy-start | bytes 3145732
  2.5 1.6 %copy-start.2 = (bf16[2,2,1024,256]{3,2,1,0:T(8,128)(2,1)S(1)}, bf16[2,2,1024,256]{3,2,1,0:T(8,128)(2,1)}, u32[]{:S(2)}) copy-start(bf16[2,2,1024,256]{3,2,1,0:T(8,128)(2,1)} %constant.7.clone.y_hbm) | copy-start | bytes 6291460
  4.0 1.0 %copy-start.3 = (bf16[2,2,512,128]{3,2,1,0:T(8,128)(2,1)S(1)}, bf16[2,2,512,128]{3,2,1,0:T(8,128)(2,1)}, u32[]{:S(2)}) copy-start(bf16[2,2,512,128]{3,2,1,0:T(8,128)(2,1)} %constant.8.clone.h_hbm) | copy-start | bytes 1572868
  5.1 0.9 %copy-start.4 = (bf16[4,128,192]{2,1,0:T(8,128)(2,1)S(1)}, bf16[4,128,192]{2,1,0:T(8,128)(2,1)}, u32[]{:S(2)}) copy-start(bf16[4,128,192]{2,1,0:T(8,128)(2,1)} %constant.6.clone.x_hbm) | copy-start | bytes 589828

commit v2 on v1

--- a/solution.py
+++ b/solution.py
@@ -12,6 +12,8 @@
 
 MESH = pl.DeviceIdType.MESH
 REACH = 16
+FINE = 8
+SENT = 6
 GROUP = 8
 LANES = 128
 
@@ -26,10 +28,14 @@
     return a
 
 
+def factors(n):
+    r = np.kron(np.eye(n // 2), np.ones((1, 2))) / math.sqrt(2.0)
+    return smoothing(n), smoothing(n // 2), r
+
+
 def four_terms(n):
-    a = smoothing(n)
-    r = np.kron(np.eye(n // 2), np.ones((1, 2))) / math.sqrt(2.0)
-    b = r.T @ smoothing(n // 2) @ r
+    a, small, r = factors(n)
+    b = r.T @ small @ r
     return [a @ a, a @ b, b @ a, b @ b]
 
 
@@ -39,16 +45,68 @@
     return hi, lo
 
 
-def constants(nx, ny, gx, gy):
-    rows, cols = nx // gx, ny // gy
-    xs = []
+def triple(m):
+    hi, lo = split_np(m)
+    return np.concatenate([hi, lo, hi], 1)
+
+
+def window(m, g, rows, margin):
+    wide = np.pad(m, ((0, 0), (margin, margin)))
+    return wide[g * rows : (g + 1) * rows, g * rows : (g + 1) * rows + 2 * margin]
+
+
+def x_constants(nx, gx):
+    rows = nx // gx
+    crows = rows // 2
+    a, small, r = factors(nx)
+    terms = four_terms(nx)
+    coarse_a = r @ a
+    spread = r.T @ small
+    main, full, extra, sender = [], [], [], []
     for g in range(gx):
+        full.append(triple(np.concatenate([window(m, g, rows, REACH) for m in terms], 0)))
+        keep = np.zeros(nx // 2)
+        keep[max(0, g * crows - 2) : (g + 1) * crows + 2] = 1.0
+        near = [terms[0], terms[1], spread @ (keep[:, None] * coarse_a), terms[3]]
+        main.append(triple(np.concatenate([window(m, g, rows, FINE) for m in near], 0)))
         blocks = []
-        for m in four_terms(nx):
-            wide = np.pad(m, ((0, 0), (REACH, REACH)))
-            blocks.append(wide[g * rows : (g + 1) * rows, g * rows : (g + 1) * rows + 2 * REACH])
-        hi, lo = split_np(np.concatenate(blocks, 0))
-        xs.append(np.concatenate([hi, lo, hi], 1))
+        at_v = [range(g * crows - 8, g * crows - 4), range((g + 1) * crows + 4, (g + 1) * crows + 8)]
+        at_w = [range(g * crows - 4, g * crows - 2), range((g + 1) * crows + 2, (g + 1) * crows + 4)]
+        for m, is_v in ((a @ spread, True), (r.T @ small @ small, True), (spread, False)):
+            e = np.zeros((rows, 16))
+            for side in range(2):
+                for n, q in enumerate(at_v[side] if is_v else at_w[side]):
+                    if 0 <= q < nx // 2:
+                        e[:, side * 8 + n + (0 if is_v else 4)] = m[g * rows : (g + 1) * rows, q]
+            blocks.append(e)
+        extra.append(triple(np.concatenate(blocks, 0)))
+        mine = slice(g * rows, (g + 1) * rows)
+        s = np.zeros((16, rows))
+        low = g * crows
+        s[0:4] = r[low + 4 : low + 8, mine]
+        s[4:6] = coarse_a[low + 2 : low + 4, mine]
+        top = (g + 1) * crows
+        s[8:12] = r[top - 8 : top - 4, mine]
+        s[12:14] = coarse_a[top - 4 : top - 2, mine]
+        sender.append(triple(s))
+    return [np.stack(m) for m in (main, full, extra, sender)]
+
+
+def y_constants(ny, gy):
+    cols = ny // gy
+    a, small, r = factors(ny)
+    extra, sender = [], []
+    for g in range(gy):
+        mine, coarse = slice(g * cols, (g + 1) * cols), slice(g * cols // 2, (g + 1) * cols // 2)
+        parts = [a @ r.T @ small, r.T @ small @ small, r.T]
+        extra.append(np.stack(split_np(np.concatenate([m[mine, coarse].T for m in parts], 0))))
+        parts = [r, small @ r @ a]
+        sender.append(np.stack(split_np(np.concatenate([m[coarse, mine].T for m in parts], 1))))
+    return np.stack(extra), np.stack(sender)
+
+
+def constants(ny, gy):
+    cols = ny // gy
     ys, hs = [], []
     for g in range(gy):
         own, edge = [], []
@@ -67,7 +125,7 @@
             edge.append(block)
         ys.append(np.stack(split_np(np.concatenate(own, 0))))
         hs.append(np.stack(split_np(np.concatenate(edge, 0))))
-    return np.stack(xs), np.stack(ys), np.stack(hs)
+    return np.stack(ys), np.stack(hs)
 
 
 def split(v):
@@ -81,9 +139,9 @@
 
 def kernel(
     gx_n, scale, chunks, per_chunk,
-    p_hbm, c_hbm, x_hbm, y_hbm, h_hbm, out_hbm,
-    p, c, f, pk, hk, xm, ym, hm, con, ra, rb, ob,
-    ld, kd, zs, zr, ds, dr, as_, ar, bs, br, od,
+    p_hbm, c_hbm, sx_hbm, sy_hbm, x_hbm, xh_hbm, xe_hbm, y_hbm, h_hbm, ye_hbm, out_hbm,
+    p, c, f, pk, hk, es, ex, sx, sy, xm, xh, xe, ym, hm, ye, con, ra, rb, ob,
+    ld, kd, zs, zr, es_, er, ds, dr, as_, ar, bs, br, od,
 ):
     half = p.shape[0]
     rows, cols = p.shape[3], p.shape[4]
@@ -100,18 +158,24 @@
             for n, (src, dst) in enumerate(((p_hbm, p), (c_hbm, c)))
         ]
 
-    def const_loads():
+    def const_loads(which):
+        pairs = (
+            (sx_hbm, sx, gx), (sy_hbm, sy, gy), (x_hbm, xm, gx), (xh_hbm, xh, gx),
+            (xe_hbm, xe, gx), (y_hbm, ym, gy), (h_hbm, hm, gy), (ye_hbm, ye, gy),
+        )
         return [
-            pltpu.make_async_copy(x_hbm.at[gx], xm, kd.at[0]),
-            pltpu.make_async_copy(y_hbm.at[gy], ym, kd.at[1]),
-            pltpu.make_async_copy(h_hbm.at[gy], hm, kd.at[2]),
+            pltpu.make_async_copy(pairs[n][0].at[pairs[n][2]], pairs[n][1], kd.at[n]) for n in which
         ]
 
-    for k in range(chunks):
+    for copy in loads(0) + const_loads((0, 1)):
+        copy.start()
+    for k in range(1, chunks):
         for copy in loads(k):
             copy.start()
-    for copy in const_loads():
+    for copy in const_loads(range(2, 8)):
         copy.start()
+
+    ex[...] = jnp.zeros_like(ex)
 
     barrier = pltpu.get_barrier_semaphore()
     greet = lambda where: pl.semaphore_signal(barrier, inc=1, device_id=where, device_id_type=MESH)
@@ -132,12 +196,12 @@
 
     @pl.when(gx == 0)
     def _():
-        f[:, :, :, 0:REACH] = jnp.zeros_like(f[:, :, :, 0:REACH])
+        f[:, :, :, 0:FINE] = jnp.zeros_like(f[:, :, :, 0:FINE])
         hk[:, :, 0:REACH] = jnp.zeros_like(hk[:, :, 0:REACH])
 
     @pl.when(gx == gx_n - 1)
     def _():
-        f[:, :, :, rows + REACH :] = jnp.zeros_like(f[:, :, :, rows + REACH :])
+        f[:, :, :, rows + FINE :] = jnp.zeros_like(f[:, :, :, rows + FINE :])
         hk[:, :, rows + REACH :] = jnp.zeros_like(hk[:, :, rows + REACH :])
 
     pl.semaphore_wait(
@@ -146,7 +210,9 @@
     )
 
     low, high = pl.ds(0, REACH), pl.ds(rows + REACH, REACH)
-    first, last = pl.ds(REACH, REACH), pl.ds(rows, REACH)
+    f_low, f_high = pl.ds(0, FINE), pl.ds(rows + FINE, FINE)
+    first, last = pl.ds(FINE, FINE), pl.ds(rows, FINE)
+    e_low, e_high = pl.ds(0, SENT), pl.ds(8, SENT)
 
     def remote(src, dst, ss, rs, where):
         return pltpu.make_async_remote_copy(
@@ -160,13 +226,15 @@
 
     def down(k):
         return (
-            remote(f.at[:, :, part(k), first], f.at[:, :, part(k), high], zs.at[k, 0], zr.at[k, 0], {"gx": gx - 1}),
+            remote(f.at[:, :, part(k), first], f.at[:, :, part(k), f_high], zs.at[k, 0], zr.at[k, 0], {"gx": gx - 1}),
+            remote(es.at[k, :, e_low], ex.at[k, :, e_high], es_.at[k, 0], er.at[k, 0], {"gx": gx - 1}),
             remote(pk.at[k, :, pl.ds(0, REACH)], hk.at[k, :, high], ds.at[k, 1], dr.at[k, 1], {"gx": gx - 1, "gy": other}),
         )
 
     def up(k):
         return (
-            remote(f.at[:, :, part(k), last], f.at[:, :, part(k), low], zs.at[k, 1], zr.at[k, 1], {"gx": gx + 1}),
+            remote(f.at[:, :, part(k), last], f.at[:, :, part(k), f_low], zs.at[k, 1], zr.at[k, 1], {"gx": gx + 1}),
+            remote(es.at[k, :, e_high], ex.at[k, :, e_low], es_.at[k, 1], er.at[k, 1], {"gx": gx + 1}),
             remote(pk.at[k, :, pl.ds(rows - REACH, REACH)], hk.at[k, :, low], ds.at[k, 2], dr.at[k, 2], {"gx": gx + 1, "gy": other}),
         )
 
@@ -174,21 +242,33 @@
     groups = [members[n : n + GROUP] for n in range(0, len(members), GROUP)]
     slot = lax.broadcasted_iota(jnp.int32, (rows, LANES), 1) // REACH
     moved = jnp.where(gy == 0, GROUP - 1, 0)
+    is_v = lax.rem(lax.broadcasted_iota(jnp.int32, (GROUP * 16, cols // 2), 0), 8) < 4
+
+    for copy in const_loads((0, 1)):
+        copy.wait()
 
     def send(k, carry):
         for copy in loads(k):
             copy.wait()
         for n, group in enumerate(groups):
             packed = jnp.zeros((rows, LANES), jnp.float32)
+            made = []
             for s, (i, b, j) in enumerate(group):
                 at = k * per_chunk + j
                 v = p[i, b, at] * c[i, b, at]
-                f[i, b, at, pl.ds(REACH, rows)] = v
+                f[i, b, at, pl.ds(FINE, rows)] = v
+                hi, lo = split(v)
+                made.append(dot(sx[...], jnp.concatenate([hi, hi, lo], 0)))
                 edge = jnp.where(gy == 0, v[:, cols - LANES :], v[:, :LANES])
                 if s:
                     edge = pltpu.roll(edge, s * REACH, 1)
                 packed = jnp.where(slot == lax.rem(s + moved, GROUP), edge, packed)
             pk[k, n] = packed
+            hi, lo = split(jnp.concatenate(made, 0))
+            made = dot(hi, sy[0]) + dot(lo, sy[0]) + dot(hi, sy[1])
+            made = jnp.where(is_v, made[:, : cols // 2], made[:, cols // 2 :])
+            for s in range(GROUP):
+                es[k, n * GROUP + s] = made[s * 16 : (s + 1) * 16]
 
         @pl.when(gx > 0)
         def _():
@@ -204,7 +284,7 @@
         return carry
 
     lax.fori_loop(0, chunks, send, 0)
-    for copy in const_loads():
+    for copy in const_loads(range(2, 8)):
         copy.wait()
 
     def to_core(k):
@@ -230,23 +310,28 @@
                 copy.wait_recv()
 
         side(k).wait_recv()
-        x = xm[...]
         for n, group in enumerate(groups):
-            his, los = [], []
-
-            def along_x(v):
+            his, los, ehis, elos = [], [], [], []
+
+            def along_x(m, v):
                 hi, lo = split(v)
-                g = dot(x, jnp.concatenate([hi, hi, lo], 0))
-                g = jnp.concatenate([g[t * rows : (t + 1) * rows] for t in range(4)], 1)
+                g = dot(m, jnp.concatenate([hi, hi, lo], 0))
+                terms = m.shape[0] // rows
+                g = jnp.concatenate([g[t * rows : (t + 1) * rows] for t in range(terms)], 1)
                 return split(g)
 
-            for i, b, j in group:
-                hi, lo = along_x(f[i, b, k * per_chunk + j])
+            for s, (i, b, j) in enumerate(group):
+                hi, lo = along_x(xm[...], f[i, b, k * per_chunk + j])
                 his.append(hi)
                 los.append(lo)
+                hi, lo = along_x(xe[...], ex[k, n * GROUP + s])
+                ehis.append(hi)
+                elos.append(lo)
             hi, lo = jnp.concatenate(his, 0), jnp.concatenate(los, 0)
             res = dot(hi, ym[0]) + dot(lo, ym[0]) + dot(hi, ym[1])
-            hi, lo = along_x(hk[k, n])
+            hi, lo = jnp.concatenate(ehis, 0), jnp.concatenate(elos, 0)
+            res = res + (dot(hi, ye[0]) + dot(lo, ye[0]) + dot(hi, ye[1]))
+            hi, lo = along_x(xh[...], hk[k, n])
             edge = dot(hi, hm[0]) + dot(lo, hm[0]) + dot(hi, hm[1])
             for s, (i, b, j) in enumerate(group):
                 at = k * per_chunk + j
@@ -320,7 +405,10 @@
     per_chunk = next(n for n in range(1, per + 1) if per % n == 0 and mem * n % GROUP == 0)
     chunks = per // per_chunk
     n_groups = mem * per_chunk // GROUP
-    xm, ym, hm = constants(rows * gx, cols * gy, gx, gy)
+    xm, xh, xe, sx = x_constants(rows * gx, gx)
+    ym, hm = constants(cols * gy, gy)
+    ye, sy = y_constants(cols * gy, gy)
+    fixed = (sx, sy, xm, xh, xe, ym, hm, ye)
     shape = (half, 2, per, rows, cols)
     tall = rows + 2 * REACH
     f32 = jnp.float32
@@ -330,23 +418,25 @@
     out = pl.pallas_call(
         functools.partial(kernel, gx, 1.0 / (mem * members - 1), chunks, per_chunk),
         out_shape=jax.ShapeDtypeStruct((per, rows, cols), f32),
-        in_specs=[any_] * 5,
+        in_specs=[any_] * (2 + len(fixed)),
         out_specs=any_,
         scratch_shapes=[
             pltpu.VMEM(shape, f32),
             pltpu.VMEM(shape, f32),
-            pltpu.VMEM((half, 2, per, tall, cols), f32),
+            pltpu.VMEM((half, 2, per, rows + 2 * FINE, cols), f32),
             pltpu.VMEM((chunks, n_groups, rows, LANES), f32),
             pltpu.VMEM((chunks, n_groups, tall, LANES), f32),
-            pltpu.VMEM(xm.shape[1:], jnp.bfloat16),
-            pltpu.VMEM(ym.shape[1:], jnp.bfloat16),
-            pltpu.VMEM(hm.shape[1:], jnp.bfloat16),
+            pltpu.VMEM((chunks, n_groups * GROUP, 16, cols // 2), f32),
+            pltpu.VMEM((chunks, n_groups * GROUP, 16, cols // 2), f32),
+            *[pltpu.VMEM(m.shape[1:], jnp.bfloat16) for m in fixed],
             pltpu.VMEM(shape, f32),
             pltpu.VMEM((half, per, rows, cols), f32),
             pltpu.VMEM((n_to, per, rows, cols), f32),
             pltpu.VMEM((per, rows, cols), f32),
             dma((chunks, 2)),
-            dma((3,)),
+            dma((len(fixed),)),
+            dma((chunks, 2)),
+            dma((chunks, 2)),
             dma((chunks, 2)),
             dma((chunks, 2)),
             dma((chunks, 3)),
@@ -358,15 +448,13 @@
             dma((chunks,)),
         ],
         compiler_params=pltpu.CompilerParams(
-            collective_id=0, has_side_effects=True, vmem_limit_bytes=40 * 1024 * 1024
+            collective_id=0, has_side_effects=True, vmem_limit_bytes=63 * 1024 * 1024
         ),
         cost_estimate=pl.CostEstimate(flops=10**10, bytes_accessed=4 * 2**20, transcendentals=0),
     )(
         perturbations.reshape(shape),
         control.reshape(shape),
-        jnp.asarray(xm),
-        jnp.asarray(ym),
-        jnp.asarray(hm),
+        *[jnp.asarray(m) for m in fixed],
     )
     return out
 

time: 32.3 us -> 24.8 us (0.77)
  local copies, waits for them, and re-layouts: 6.73 us -> 1.67 us
  Pallas kernels: 25.3 us -> 23 us
    unnamed x11 -> x1, local copies, waits for them, and re-layouts: 6.73 us -> 1.67 us
    pallas_call x1, Pallas kernels: 25.3 us -> 23 us  [body(): pl.pallas_call(functools.partial(kernel, gx, 1.0 / (mem * members - 1), c...]
where the time goes in v2:
time: 24.8 us; the launch traced here: 24.7 us
  Pallas kernels  23 us (93%)
  local copies, waits for them, and re-layouts  1.67 us (7%)
    pallas_call x1, Pallas kernels, body(): pl.pallas_call(functools.partial(kernel, gx, 1.0 / (mem * members - 1), c...  23 us
    unnamed x1, local copies, waits for them, and re-layouts  1.67 us

profile of v2, /device:TPU:0, one launch (start us, length us, event | category | flops | bytes accessed | tf_op | source)
XLA Modules:
  0.0 24.7 jit_solution(11497540055908952565)
XLA Ops:
  0.0 23.0 %shard_map.100 = f32[8,32,256]{2,1,0:T(8,128)} custom-call(f32[2,2,8,32,256]{4,3,2,1,0:T(8,128)} %bitcast.2, f32[2,2,8,32,256]{4,3,2,1,0:T(8,128)} %bitcast.3, bf16[4,16,96]{2,1,0:T(8,128)(2,1)} %constant.16.clone.sx_hbm, bf16[2,2,256,256]{3,2,1,0:T(8,128)(2,1)} %constant.17.clone.sy_hbm, bf16[4,128,144]{2,1,0:T(8,128)(2,1)} %constant.18.clone.x_hbm, ...), custom_call_target="tpu_custom_call" | custom-call | flops 10000000000 | bytes 4194304 | tf_op jit(solution)/shard_map/pallas_call | solution.py:418
  23.0 1.7 %copy.12 = f32[8,32,256]{2,1,0:T(8,128)} copy(f32[8,32,256]{2,1,0:T(8,128)} %shard_map.100) | data formatting | bytes 524288

commit v3 on v2

--- a/solution.py
+++ b/solution.py
@@ -247,40 +247,45 @@
     for copy in const_loads((0, 1)):
         copy.wait()
 
+    def start(k, which):
+        @pl.when(gx > 0)
+        def _():
+            for n in which:
+                down(k)[n].start()
+
+        @pl.when(gx < gx_n - 1)
+        def _():
+            for n in which:
+                up(k)[n].start()
+
     def send(k, carry):
         for copy in loads(k):
             copy.wait()
         for n, group in enumerate(groups):
             packed = jnp.zeros((rows, LANES), jnp.float32)
-            made = []
             for s, (i, b, j) in enumerate(group):
                 at = k * per_chunk + j
                 v = p[i, b, at] * c[i, b, at]
                 f[i, b, at, pl.ds(FINE, rows)] = v
-                hi, lo = split(v)
-                made.append(dot(sx[...], jnp.concatenate([hi, hi, lo], 0)))
                 edge = jnp.where(gy == 0, v[:, cols - LANES :], v[:, :LANES])
                 if s:
                     edge = pltpu.roll(edge, s * REACH, 1)
                 packed = jnp.where(slot == lax.rem(s + moved, GROUP), edge, packed)
             pk[k, n] = packed
+
+        start(k, (0, 2))
+        side(k).start()
+        for n, group in enumerate(groups):
+            made = []
+            for i, b, j in group:
+                hi, lo = split(f[i, b, k * per_chunk + j, pl.ds(FINE, rows)])
+                made.append(dot(sx[...], jnp.concatenate([hi, hi, lo], 0)))
             hi, lo = split(jnp.concatenate(made, 0))
             made = dot(hi, sy[0]) + dot(lo, sy[0]) + dot(hi, sy[1])
             made = jnp.where(is_v, made[:, : cols // 2], made[:, cols // 2 :])
-            for s in range(GROUP):
+            for s in range(len(group)):
                 es[k, n * GROUP + s] = made[s * 16 : (s + 1) * 16]
-
-        @pl.when(gx > 0)
-        def _():
-            for copy in down(k):
-                copy.start()
-
-        @pl.when(gx < gx_n - 1)
-        def _():
-            for copy in up(k):
-                copy.start()
-
-        side(k).start()
+        start(k, (1,))
         return carry
 
     lax.fori_loop(0, chunks, send, 0)

time: 24.8 us -> 24.6 us (level)
  no operation moved by 1% of the time
where the time goes in v3:
time: 24.6 us; the launch traced here: 24.5 us
  Pallas kernels  22.8 us (93%)
  local copies, waits for them, and re-layouts  1.67 us (7%)
    pallas_call x1, Pallas kernels, body(): pl.pallas_call(functools.partial(kernel, gx, 1.0 / (mem * members - 1), c...  22.8 us
    unnamed x1, local copies, waits for them, and re-layouts  1.67 us

profile of v3, /device:TPU:0, one launch (start us, length us, event | category | flops | bytes accessed | tf_op | source)
XLA Modules:
  0.0 24.5 jit_solution(1087873334841059832)
XLA Ops:
  0.0 22.8 %shard_map.100 = f32[8,32,256]{2,1,0:T(8,128)} custom-call(f32[2,2,8,32,256]{4,3,2,1,0:T(8,128)} %bitcast.2, f32[2,2,8,32,256]{4,3,2,1,0:T(8,128)} %bitcast.3, bf16[4,16,96]{2,1,0:T(8,128)(2,1)} %constant.16.clone.sx_hbm, bf16[2,2,256,256]{3,2,1,0:T(8,128)(2,1)} %constant.17.clone.sy_hbm, bf16[4,128,144]{2,1,0:T(8,128)(2,1)} %constant.18.clone.x_hbm, ...), custom_call_target="tpu_custom_call" | custom-call | flops 10000000000 | bytes 4194304 | tf_op jit(solution)/shard_map/pallas_call | solution.py:423
  22.8 1.7 %copy.12 = f32[8,32,256]{2,1,0:T(8,128)} copy(f32[8,32,256]{2,1,0:T(8,128)} %shard_map.100) | data formatting | bytes 524288
